TPU v7x, 32 devices: a whole 2x2x4 slice. The times are simulated.
32 devices in a mesh: groups: 2 (over x), seq: 8 (over z, y), mp: 2 (over core).
Axes of the slice: x: 2, y: 2, z: 4, core: 2. Of those that a mesh axis runs over, the one named last changes fastest.
Arguments:
- hidden: bfloat16 [4, 2048, 512], P('groups', 'seq'), parts along dimension 0, may hold values from -6 to 6
- in_weight: bfloat16 [512, 2304], replicated, may hold values from -0.25 to 0.25
- dt_weight: bfloat16 [512, 16], replicated, may hold values from -0.25 to 0.25
- conv_weight: float32 [2, 4, 1280], replicated, may hold values from -3 to 3
- dt_bias: float32 [2, 16], replicated, may hold values from -2 to 1
- decay_rate: float32 [2, 16], replicated, may hold values from 9.765625e-06 to 0.05
- skip_gain: float32 [2, 16], replicated, may hold values from 0.5 to 1.5
- norm_gain: float32 [2, 1024], replicated, may hold values from 0.5 to 1.5
- out_weight: bfloat16 [1024, 512], replicated, may hold values from -0.1875 to 0.1875
Outputs:
- strands_out: bfloat16 [4, 2048, 1024], P('groups', 'seq', 'mp'), parts along dimension 0
There are 2 independent parts, one for each index of `groups`. A program takes and returns all parts, laid end to end along the dimension named above; an argument that names none is the same for every part. Nothing has to cross between parts.
All inputs are finite; a program needn't handle non-finite values.
Results may differ from a plain program's by a relative error of at most 0.0051.
Values may be sent and summed in bfloat16 or wider, within the bound.
A program may use at most 256 MiB of HBM per device.

v0:
```python
import jax
import jax.numpy as jnp
from jax import lax
from jax.sharding import PartitionSpec as P

HEADS = 16
HEAD_DIM = 64
STATE = 128
SPAN = 256
CONV = 4
INNER = 1024


epsilon = 1e-05


def swapped(shard, axis, bit):
    return lax.ppermute(shard, axis, [(i, i ^ 1 << bit) for i in range(lax.axis_size(axis))])


def padded_2(shard, sides, width):
    for axis, dim in sides:
        devices, length = (lax.axis_size(axis), shard.shape[dim])
        up = [(i, (i + 1) % devices) for i in range(devices - 1)]
        down = [(j, i) for i, j in up]
        last = lax.slice_in_dim(shard, length - width, length, axis=dim)
        leading = lax.slice_in_dim(shard, 0, width, axis=dim)
        before = lax.ppermute(last, axis, up)
        after = lax.ppermute(leading, axis, down)
        shard = jnp.concatenate([before, shard, after], axis=dim)
    return shard


def entering(value, axis, join, neutral, backward):
    count, mine = (lax.axis_size(axis), lax.axis_index(axis))
    pieces = jax.tree.map(lambda part: lax.all_gather(part, axis), value)
    if backward:
        pieces = jax.tree.map(lambda part: part[::-1], pieces)
        mine = count - 1 - mine
    running = jax.tree.map(
        lambda part, zero: jnp.full_like(part, 0) + jnp.asarray(zero, part.dtype), value, neutral
    )

    def hop(position, running):
        longer = join(running, jax.tree.map(lambda part: part[position], pieces))
        return jax.tree.map(lambda new, old: jnp.where(position < mine, new, old), longer, running)

    return lax.fori_loop(0, count - 1, hop, running)


def span_scan(x_rows, b_rows, c_rows, dt_rows, log_rows, initial):
    block_count = x_rows.shape[0] // SPAN
    head_count = dt_rows.shape[1]
    head_width = x_rows.shape[1] // head_count
    causal = jnp.arange(SPAN)[:, None] >= jnp.arange(SPAN)[None, :]

    def advance(carried, pieces):
        x_part, b_part, c_part, dt_part, log_part = pieces
        running = jnp.cumsum(log_part, axis=0)
        scores = jnp.dot(c_part, b_part.T, preferred_element_type=jnp.float32)
        spread = running.T[:, :, None] - running.T[:, None, :]
        mixing = jnp.where(
            causal,
            scores[None] * jnp.exp(jnp.where(causal, spread, 0.0)) * dt_part.T[:, None, :],
            0.0,
        ).astype(jnp.bfloat16)
        heads_x = x_part.reshape(SPAN, head_count, head_width)
        within = jnp.einsum("hts,shp->thp", mixing, heads_x, preferred_element_type=jnp.float32)
        across = jnp.exp(running)[:, :, None] * jnp.einsum(
            "tn,hpn->thp", c_part.astype(jnp.float32), carried, precision=lax.Precision.HIGHEST
        )
        remain = jnp.exp(running[-1][None, :] - running) * dt_part
        weighted = (b_part.astype(jnp.float32)[:, None, :] * remain[:, :, None]).astype(
            jnp.bfloat16
        )
        contrib = jnp.einsum("shn,shp->hpn", weighted, heads_x, preferred_element_type=jnp.float32)
        carried = jnp.exp(running[-1])[:, None, None] * carried + contrib
        return (carried, (within + across).reshape(SPAN, head_count * head_width))

    pieces = tuple(
        (
            member.reshape(block_count, SPAN, member.shape[1])
            for member in (x_rows, b_rows, c_rows, dt_rows, log_rows)
        )
    )
    final_state, outputs = lax.scan(advance, initial, pieces)
    return (outputs.reshape(block_count * SPAN, head_count * head_width), final_state)


def chain_join(earlier, latter):
    return (earlier[0] + latter[0], jnp.exp(latter[0])[..., None, None] * earlier[1] + latter[1])


def select_tree(flag, first_tree, second_tree):
    return jax.tree.map(
        lambda first_arr, second_arr: jnp.where(flag, first_arr, second_arr),
        first_tree,
        second_tree,
    )


def on_device(
    hidden, in_weight, dt_weight, conv_weight, dt_bias, decay_rate, skip_gain, norm_gain, out_weight
):
    seq_count = lax.axis_size("seq")
    bit_count = seq_count.bit_length() - 1
    is_reverse = lax.axis_index("mp") == 1
    mirror_in = hidden
    for bit_level in range(bit_count):
        mirror_in = swapped(mirror_in, "seq", bit_level)
    inputs = jnp.where(is_reverse, mirror_in[:, ::-1], hidden)
    rising = jnp.logical_not(False)
    projected = jnp.einsum("std,de->ste", inputs, in_weight, preferred_element_type=jnp.float32)
    gating = projected[..., :INNER]
    mixed_in = projected[..., INNER:].astype(jnp.bfloat16)
    dt_raw = jnp.einsum("std,dh->sth", inputs, dt_weight, preferred_element_type=jnp.float32)
    padded = padded_2(mixed_in, (("seq", 1),), CONV - 1)
    gating = jnp.where(False, gating[:, ::-1], gating)
    dt_raw = jnp.where(False, dt_raw[:, ::-1], dt_raw)
    padded = jnp.where(False, padded[:, ::-1], padded)
    row_count = gating.shape[1]
    seq_local = gating.shape[0]
    scan_batch = jax.vmap(span_scan, in_axes=(0, 0, 0, 0, 0, None))
    empty_state = jnp.zeros((HEADS, HEAD_DIM, STATE), jnp.float32)
    partial_list = []
    for direction in range(2):
        ordered = padded if direction == 0 else padded[:, ::-1]
        source = ordered.astype(jnp.float32)
        convolved = conv_weight[direction, 0] * source[:, 0:row_count]
        for offset in range(1, CONV):
            convolved = (
                convolved + conv_weight[direction, offset] * source[:, offset : offset + row_count]
            )
        activated = jax.nn.silu(convolved).astype(jnp.bfloat16)
        x_rows = activated[..., :INNER]
        b_rows = activated[..., INNER : INNER + STATE]
        c_rows = activated[..., INNER + STATE :]
        dt_source = dt_raw if direction == 0 else dt_raw[:, ::-1]
        dt_step = jax.nn.softplus(dt_source + dt_bias[direction])
        log_decay = -dt_step * decay_rate[direction]
        local_out, final_state = scan_batch(x_rows, b_rows, c_rows, dt_step, log_decay, empty_state)
        partial_list.append(
            (
                local_out,
                c_rows,
                jnp.cumsum(log_decay, axis=1),
                x_rows,
                jnp.sum(log_decay, axis=1),
                final_state,
            )
        )
    neutral = (
        jnp.zeros((seq_local, HEADS), jnp.float32),
        jnp.zeros((seq_local, HEADS, HEAD_DIM, STATE), jnp.float32),
    )
    forth = (partial_list[0][4], partial_list[0][5])
    backward = (partial_list[1][4], partial_list[1][5])
    upward = entering(select_tree(rising, forth, backward), "seq", chain_join, neutral, False)
    downward = entering(select_tree(rising, backward, forth), "seq", chain_join, neutral, True)
    entries = (select_tree(rising, upward, downward)[1], select_tree(rising, downward, upward)[1])
    silu_gate = jax.nn.silu(gating)
    summed = jnp.zeros(gating.shape, jnp.float32)
    for direction in range(2):
        local_out, c_rows, running, x_rows = partial_list[direction][:4]
        carried_in = jnp.einsum(
            "stn,shpn->sthp",
            c_rows.astype(jnp.float32),
            entries[direction],
            precision=lax.Precision.HIGHEST,
        )
        result_rows = local_out + (jnp.exp(running)[..., None] * carried_in).reshape(
            local_out.shape
        )
        result_rows = result_rows + jnp.repeat(skip_gain[direction], HEAD_DIM) * x_rows.astype(
            jnp.float32
        )
        if direction == 1:
            result_rows = result_rows[:, ::-1]
        gated = result_rows * silu_gate
        gated = (
            gated
            * lax.rsqrt(jnp.mean(gated * gated, axis=-1, keepdims=True) + epsilon)
            * norm_gain[direction]
        )
        summed = summed + gated
    mixed_out = jnp.einsum(
        "ste,ed->std", summed.astype(jnp.bfloat16), out_weight, preferred_element_type=jnp.float32
    ).astype(jnp.bfloat16)
    mirror_out = mixed_out[:, ::-1]
    for bit_level in range(bit_count):
        mirror_out = swapped(mirror_out, "seq", bit_level)
    finished = jnp.where(is_reverse, mirror_out, mixed_out)
    return finished


def solution(mesh):
    in_specs = (P("groups", "seq", None), P(), P(), P(), P(), P(), P(), P(), P())
    out_specs = P("groups", "seq", "mp")
    return jax.shard_map(
        on_device, mesh=mesh, in_specs=in_specs, out_specs=out_specs, check_vma=False
    )
```

profile of v0, /device:TPU:4, one launch (start us, length us, event | category | flops | bytes accessed | tf_op | source)
XLA Modules:
  0.0 454.9 jit_solution(6225095250681916510)
XLA Ops:
  6.5 13.9 %collective-permute-done = bf16[2,256,512]{2,1,0:T(8,128)(2,1)S(1)} collective-permute-done((bf16[2,256,512]{2,1,0:T(8,128)(2,1)}, bf16[2,256,512]{2,1,0:T(8,128)(2,1)S(1)}, u32[]{:S(2)}, u32[]{:S(2)}) %collective-permute-start) | collective-permute-done | bytes 524320 | tf_op jit(solution)/shard_map/ppermute | solution.py:18
  22.0 11.2 %collective-permute-done.1 = bf16[2,256,512]{2,1,0:T(8,128)(2,1)S(1)} collective-permute-done((bf16[2,256,512]{2,1,0:T(8,128)(2,1)S(1)}, bf16[2,256,512]{2,1,0:T(8,128)(2,1)S(1)}, u32[]{:S(2)}, u32[]{:S(2)}) %collective-permute-start.1) | collective-permute-done | bytes 524320 | tf_op jit(solution)/shard_map/ppermute | solution.py:18
  40.0 17.2 %collective-permute-done.2 = bf16[2,256,512]{2,1,0:T(8,128)(2,1)S(1)} collective-permute-done((bf16[2,256,512]{2,1,0:T(8,128)(2,1)S(1)}, bf16[2,256,512]{2,1,0:T(8,128)(2,1)S(1)}, u32[]{:S(2)}, u32[]{:S(2)}) %collective-permute-start.2) | collective-permute-done | bytes 524320 | tf_op jit(solution)/shard_map/ppermute | solution.py:18
  67.8 3.6 fusion.80
  74.0 3.3 collective-permute-start.4
  82.0 28.1 %rev.25 = bf16[2,262,1280]{2,1,0:T(8,128)(2,1)} reverse(bf16[2,262,1280]{2,1,0:T(8,128)(2,1)} %get-tuple-element.320), dimensions={1} | reverse | bytes 2682880 | tf_op jit(solution)/shard_map/rev | solution.py:127
  111.9 4.2 multiply_convert_fusion.2
  121.8 3.8 fusion.33
  126.0 17.2 %all-gather.5 = f32[8,2,16]{2,1,0:T(2,128)S(1)} all-gather(f32[1,2,16]{2,1,0:T(2,128)S(1)} %bitcast.156), channel_id=4, replica_groups=mesh['groups'=2,'seq'=8,'mp'=2] {'seq'}, dimensions={0}, use_global_device_ids=true | all-gather | bytes 1152 | tf_op jit(solution)/shard_map/all_gather | solution.py:36
  143.2 19.1 %all-gather.4 = f32[8,2,16]{2,1,0:T(2,128)S(1)} all-gather(f32[1,2,16]{2,1,0:T(2,128)S(1)} %bitcast.155), channel_id=2, replica_groups=mesh['groups'=2,'seq'=8,'mp'=2] {'seq'}, dimensions={0}, use_global_device_ids=true | all-gather | bytes 1152 | tf_op jit(solution)/shard_map/all_gather | solution.py:36
  167.7 3.2 fusion.41
  170.9 74.5 %all-gather.11.cloned.1.call-done = f32[16,16,64,128]{3,2,1,0:T(8,128)} async-done(((f32[2,16,64,128]{3,2,1,0:T(8,128)}), f32[16,16,64,128]{3,2,1,0:T(8,128)}) %all-gather.11.cloned.1.call-update) | async-done | bytes 8388624 | tf_op jit(solution)/shard_map/all_gather | solution.py:36
  245.4 8.3 %rev.28 = f32[8,2,16,64,128]{4,3,2,1,0:T(8,128)} reverse(f32[8,2,16,64,128]{4,3,2,1,0:T(8,128)} %bitcast.145), dimensions={0} | reverse | bytes 16777216 | tf_op jit(solution)/shard_map/rev | solution.py:38
  253.7 10.7 %while.19 = (s32[]{:T(128)}, f32[2,16,64,128]{3,2,1,0:T(8,128)S(1)}, s32[]{:T(128)}, f32[8,2,16]{2,1,0:T(2,128)S(1)}, f32[8,2,16,64,128]{4,3,2,1,0:T(8,128)}, /*index=5*/s32[]{:T(128)}, s32[]{:T(128)}) while((s32[]{:T(128)}, f32[2,16,64,128]{3,2,1,0:T(8,128)S(1)}, s32[]{:T(128)}, f32[8,2,16]{2,1,0:T(2,128)S(1)}, ...), condition=%wide.region_10.11_spmd.clone, body=%wide.region_9.10_spmd.clone.sunk | while | flops 1048580 | bytes 3146217 | solution.py:48
  266.3 5.4 %fusion.26 = f32[2,256,16,64]{1,3,2,0:T(8,128)} fusion(f32[2,256,16,64]{1,3,2,0:T(8,128)S(1)} %fusion.45, f32[2,256,16,64]{1,3,2,0:T(8,128)S(1)} %copy-done.8, bf16[2,256,16,64]{1,3,2,0:T(8,128)(2,1)S(1)} %bitcast.152, f32[2,16,256]{2,1,0:T(8,128)S(1)} %copy-done.24, f32[2,16,256]{2,1,0:T(8,128)S(1)} %copy-done.22, f32[2,256,256]{2,1,0:T(8,128)} %fusion.51, ...), kind=kOutput, calls=%fused_computation.45 | convolution fusion | flops 283115520 | bytes 8028160 | tf_op jit(solution)/shard_map/vmap()/while/body/eval_jaxpr/hts,shp->thp/dot_general | solution.py:68
  274.6 3.4 multiply_add_fusion
  278.0 16.7 %rev.29 = f32[2,256,1024]{2,1,0:T(8,128)} reverse(f32[2,256,1024]{2,1,0:T(8,128)} %multiply_add_fusion), dimensions={1} | reverse | bytes 4194304 | tf_op jit(solution)/shard_map/rev | solution.py:178
  294.7 76.0 %all-gather.9.cloned.1.call-done = f32[16,16,64,128]{3,2,1,0:T(8,128)} async-done(((f32[2,16,64,128]{3,2,1,0:T(8,128)}), f32[16,16,64,128]{3,2,1,0:T(8,128)}) %all-gather.9.cloned.1.call-update) | async-done | bytes 8388624 | tf_op jit(solution)/shard_map/all_gather | solution.py:36
  370.7 10.6 %while.18 = (s32[]{:T(128)}, f32[2,16,64,128]{3,2,1,0:T(8,128)S(1)}, s32[]{:T(128)}, f32[8,2,16]{2,1,0:T(2,128)S(1)}, f32[8,2,16,64,128]{4,3,2,1,0:T(8,128)}, /*index=5*/s32[]{:T(128)}, s32[]{:T(128)}) while((s32[]{:T(128)}, f32[2,16,64,128]{3,2,1,0:T(8,128)S(1)}, s32[]{:T(128)}, f32[8,2,16]{2,1,0:T(2,128)S(1)}, ...), condition=%wide.region_4.5_spmd.clone, body=%wide.region_3.4_spmd.clone.sunk | while | flops 1048580 | bytes 3146217 | solution.py:48
  383.2 4.2 fusion.27
  390.3 4.1 multiply_reduce_fusion.1
  399.5 11.8 %collective-permute-done.5 = bf16[2,256,512]{2,1,0:T(8,128)(2,1)S(1)} collective-permute-done((bf16[2,256,512]{2,1,0:T(8,128)(2,1)S(1)}, bf16[2,256,512]{2,1,0:T(8,128)(2,1)S(1)}, u32[]{:S(2)}, u32[]{:S(2)}) %collective-permute-start.5) | collective-permute-done | bytes 524320 | tf_op jit(solution)/shard_map/ppermute | solution.py:18
  411.3 12.3 %collective-permute-done.6 = bf16[2,256,512]{2,1,0:T(8,128)(2,1)S(1)} collective-permute-done((bf16[2,256,512]{2,1,0:T(8,128)(2,1)S(1)}, bf16[2,256,512]{2,1,0:T(8,128)(2,1)S(1)}, u32[]{:S(2)}, u32[]{:S(2)}) %collective-permute-start.6) | collective-permute-done | bytes 524320 | tf_op jit(solution)/shard_map/ppermute | solution.py:18
  425.1 22.1 %collective-permute-done.7 = bf16[2,256,512]{2,1,0:T(8,128)(2,1)S(1)} collective-permute-done((bf16[2,256,512]{2,1,0:T(8,128)(2,1)S(1)}, bf16[2,256,512]{2,1,0:T(8,128)(2,1)S(1)}, u32[]{:S(2)}, u32[]{:S(2)}) %collective-permute-start.7) | collective-permute-done | bytes 524320 | tf_op jit(solution)/shard_map/ppermute | solution.py:18
  (169 shorter events, 77.0 us)
Async XLA Ops:
  6.5 61.3 %copy-start = (bf16[512,2304]{1,0:T(8,128)(2,1)S(1)}, bf16[512,2304]{1,0:T(8,128)(2,1)}, u32[]{:S(2)}) copy-start(bf16[512,2304]{1,0:T(8,128)(2,1)} %param.14) | copy-start | bytes 7077892
  6.5 238.9 %all-gather.11.cloned.1.call-start = ((), (), s32[]{:S(2)}) async-start(), calls=%async_computation.1 | async-start | bytes 9437184 | tf_op jit(solution)/shard_map/all_gather | solution.py:36
  6.5 13.9 %collective-permute-start = (bf16[2,256,512]{2,1,0:T(8,128)(2,1)}, bf16[2,256,512]{2,1,0:T(8,128)(2,1)S(1)}, u32[]{:S(2)}, u32[]{:S(2)}) collective-permute-start(bf16[2,256,512]{2,1,0:T(8,128)(2,1)} %param.13), channel_id=1, source_target_pairs={{0,2},{2,0},{4,6},{6,4},{8,10},{10,8},{12,14},{14,12},{1,3},{3,1},... | collective-permute-start | bytes 1572872 | tf_op jit(solution)/shard_map/ppermute | solution.py:18
  20.4 12.8 %collective-permute-start.1 = (bf16[2,256,512]{2,1,0:T(8,128)(2,1)S(1)}, bf16[2,256,512]{2,1,0:T(8,128)(2,1)S(1)}, u32[]{:S(2)}, u32[]{:S(2)}) collective-permute-start(bf16[2,256,512]{2,1,0:T(8,128)(2,1)S(1)} %collective-permute-done), channel_id=1, source_target_pairs={{0,4},{2,6},{4,0},{6,2},{8,12},{10,14},{12,8},{14,10},{1,5},{3,7},... | collective-permute-start | bytes 1572872 | tf_op jit(solution)/shard_map/ppermute | solution.py:18
  33.2 24.0 %collective-permute-start.2 = (bf16[2,256,512]{2,1,0:T(8,128)(2,1)S(1)}, bf16[2,256,512]{2,1,0:T(8,128)(2,1)S(1)}, u32[]{:S(2)}, u32[]{:S(2)}) collective-permute-start(bf16[2,256,512]{2,1,0:T(8,128)(2,1)S(1)} %collective-permute-done.1), channel_id=1, source_target_pairs={{0,8},{2,10},{4,12},{6,14},{8,0},{10,2},{12,4},{14,6},{1,9},{3,11}... | collective-permute-start | bytes 1572872 | tf_op jit(solution)/shard_map/ppermute | solution.py:18
  38.7 22.0 %copy-start.29 = (f32[16]{0:T(128)}, f32[16]{0:T(128)S(1)}, u32[]{:S(2)}) copy-start(f32[16]{0:T(128)S(1)} %get-tuple-element.339) | copy-start | bytes 196
  40.0 20.6 %copy-start.30 = (f32[16]{0:T(128)}, f32[16]{0:T(128)S(1)}, u32[]{:S(2)}) copy-start(f32[16]{0:T(128)S(1)} %get-tuple-element.341) | copy-start | bytes 196
  57.9 10.0 %copy-start.13 = (bf16[2,256,512]{2,1,0:T(8,128)(2,1)S(1)}, bf16[2,256,512]{2,1,0:T(8,128)(2,1)}, u32[]{:S(2)}) copy-start(bf16[2,256,512]{2,1,0:T(8,128)(2,1)} %param.13) | copy-start | bytes 1572868
  71.5 6.0 %collective-permute-start.3 = (bf16[2,3,1280]{2,1,0:T(4,128)(2,1)S(1)}, bf16[2,3,1280]{2,1,0:T(4,128)(2,1)S(1)}, u32[]{:S(2)}, u32[]{:S(2)}) collective-permute-start(bf16[2,3,1280]{2,1,0:T(4,128)(2,1)S(1)} %get-tuple-element.318), channel_id=1, source_target_pairs={{0,2},{2,4},{4,6},{6,8},{8,10},{10,12},{12,14},{1,3},{3,5},{5,7},{... | collective-permute-start | bytes 46088 | tf_op jit(solution)/shard_map/ppermute | solution.py:28
  74.0 6.6 %collective-permute-start.4 = (bf16[2,3,1280]{2,1,0:T(4,128)(2,1)S(1)}, bf16[2,3,1280]{2,1,0:T(4,128)(2,1)S(1)}, u32[]{:S(2)}, u32[]{:S(2)}) collective-permute-start(bf16[2,3,1280]{2,1,0:T(4,128)(2,1)S(1)} %get-tuple-element.319), channel_id=1, source_target_pairs={{2,0},{4,2},{6,4},{8,6},{10,8},{12,10},{14,12},{3,1},{5,3},{7,5},{... | collective-permute-start | bytes 46088 | tf_op jit(solution)/shard_map/ppermute | solution.py:29
  120.2 250.6 %all-gather.9.cloned.1.call-start = ((), (), s32[]{:S(2)}) async-start(), calls=%async_computation | async-start | bytes 9437184 | tf_op jit(solution)/shard_map/all_gather | solution.py:36
  121.7 3.9 copy-start.33
  121.7 4.2 copy-start.28
  121.7 4.2 copy-start.32
  121.8 21.4 %copy-start.31 = (f32[2,16]{1,0:T(2,128)S(1)}, f32[2,16]{1,0:T(2,128)}, u32[]{:S(2)}) copy-start(f32[2,16]{1,0:T(2,128)} %get-tuple-element.323) | copy-start | bytes 388
  121.8 40.5 %copy-start.3 = (bf16[2,256,1280]{2,1,0:T(8,128)(2,1)S(1)}, bf16[2,256,1280]{2,1,0:T(8,128)(2,1)}, u32[]{:S(2)}) copy-start(bf16[2,256,1280]{2,1,0:T(8,128)(2,1)} %copy-done.2) | copy-start | bytes 3932164
  370.7 10.7 %copy-start.5 = (bf16[2,256,1280]{2,1,0:T(8,128)(2,1)S(1)}, bf16[2,256,1280]{2,1,0:T(8,128)(2,1)}, u32[]{:S(2)}) copy-start(bf16[2,256,1280]{2,1,0:T(8,128)(2,1)} %get-tuple-element.349) | copy-start | bytes 3932164
  370.7 11.7 %copy-start.12 = (f32[2,256,256]{2,1,0:T(8,128)S(1)}, f32[2,256,256]{2,1,0:T(8,128)}, u32[]{:S(2)}) copy-start(f32[2,256,256]{2,1,0:T(8,128)} %fusion.53) | copy-start | bytes 1572868
  390.3 4.1 copy-start.6
  390.3 4.1 copy-start.34
  394.4 53.6 %copy-start.1 = (bf16[512,2304]{1,0:T(8,128)(2,1)S(1)}, bf16[512,2304]{1,0:T(8,128)(2,1)}, u32[]{:S(2)}) copy-start(bf16[512,2304]{1,0:T(8,128)(2,1)} %param.14) | copy-start | bytes 7077892
  397.9 13.3 %collective-permute-start.5 = (bf16[2,256,512]{2,1,0:T(8,128)(2,1)S(1)}, bf16[2,256,512]{2,1,0:T(8,128)(2,1)S(1)}, u32[]{:S(2)}, u32[]{:S(2)}) collective-permute-start(bf16[2,256,512]{2,1,0:T(8,128)(2,1)S(1)} %rev.30), channel_id=1, source_target_pairs={{0,2},{2,0},{4,6},{6,4},{8,10},{10,8},{12,14},{14,12},{1,3},{3,1},... | collective-permute-start | bytes 1572872 | tf_op jit(solution)/shard_map/ppermute | solution.py:18
  411.3 12.3 %collective-permute-start.6 = (bf16[2,256,512]{2,1,0:T(8,128)(2,1)S(1)}, bf16[2,256,512]{2,1,0:T(8,128)(2,1)S(1)}, u32[]{:S(2)}, u32[]{:S(2)}) collective-permute-start(bf16[2,256,512]{2,1,0:T(8,128)(2,1)S(1)} %collective-permute-done.5), channel_id=1, source_target_pairs={{0,4},{2,6},{4,0},{6,2},{8,12},{10,14},{12,8},{14,10},{1,5},{3,7},... | collective-permute-start | bytes 1572872 | tf_op jit(solution)/shard_map/ppermute | solution.py:18
  423.6 23.6 %collective-permute-start.7 = (bf16[2,256,512]{2,1,0:T(8,128)(2,1)S(1)}, bf16[2,256,512]{2,1,0:T(8,128)(2,1)S(1)}, u32[]{:S(2)}, u32[]{:S(2)}) collective-permute-start(bf16[2,256,512]{2,1,0:T(8,128)(2,1)S(1)} %collective-permute-done.6), channel_id=1, source_target_pairs={{0,8},{2,10},{4,12},{6,14},{8,0},{10,2},{12,4},{14,6},{1,9},{3,11}... | collective-permute-start | bytes 1572872 | tf_op jit(solution)/shard_map/ppermute | solution.py:18
  (21 other events, 38.2 us)
Sparse Core Ops, SparseCore 0:
  120.3 125.1 all-gather.10
  247.6 123.1 all-gather.8
where the time goes:
time: 462 us; the launch traced here: 455 us
  waiting for transfers between devices  242 us (52%)
  local copies, waits for them, and re-layouts  70.5 us (15%)
  other arithmetic  43.6 us (9%)
  blocking collectives  36.3 us (8%)
  matrix products  34.8 us (8%)
  between operations  14 us (3%)
  starting transfers between devices  13.1 us (3%)
    all_gather x2, waiting for transfers between devices, entering(): pieces = jax.tree.map(lambda part: lax.all_gather(part, axis), value)  151 us
    ppermute x6, waiting for transfers between devices, swapped(): lax.ppermute(shard, axis, [(i, i ^ 1 << bit) for i in range(lax.axis_size...  88.4 us
    all_gather x2, blocking collectives, entering(): pieces = jax.tree.map(lambda part: lax.all_gather(part, axis), value)  36.3 us
    rev x1, local copies, waits for them, and re-layouts, on_device(): ordered = padded if direction == 0 else padded[:, ::-1]  28.1 us
    select_n x14, other arithmetic, hop(): jnp.where(position < mine, new, old)  20.8 us
    rev x1, local copies, waits for them, and re-layouts, on_device(): result_rows = result_rows[:, ::-1]  16.7 us
    dot_general x2, matrix products, advance(): jnp.einsum('hts,shp->thp', mixing, heads_x, preferred_element_type=jnp.fl...  9.62 us
  transfers between devices with their start and end apart: 10, of which 9 were waited for; matrix products, arithmetic and copies ran while one was open for 15% of the time, Pallas kernels for 0%

commit v1 on v0

v1 whole, which is shorter than its diff:
```python
import functools

import jax
import jax.numpy as jnp
from jax import lax
from jax.experimental import pallas as pl
from jax.experimental.pallas import tpu as pltpu
from jax.sharding import PartitionSpec as P

HEADS = 16
HEAD_DIM = 64
STATE = 128
CONV = 4
INNER = 1024
MIXED = INNER + 2 * STATE
ROWS = 256
CHUNKS = 4
CHUNK_HEADS = HEADS // CHUNKS
WIDTH = INNER // CHUNKS
HALO = 16
epsilon = 1e-05

F32 = jnp.float32
BF16 = jnp.bfloat16
MESH = pl.DeviceIdType.MESH
HIGHEST = lax.Precision.HIGHEST


def silu(value):
    return value / (1.0 + jnp.exp(-value))


def dot(a, b, dims=((1,), (0,)), precision=None):
    return lax.dot_general(a, b, (dims, ((), ())), preferred_element_type=F32, precision=precision)


def column(row):
    eye = lax.broadcasted_iota(jnp.int32, (HEADS, HEADS), 0) == lax.broadcasted_iota(
        jnp.int32, (HEADS, HEADS), 1
    )
    return jnp.sum(jnp.where(eye, jnp.broadcast_to(row, (HEADS, HEADS)), 0.0), axis=1, keepdims=True)


def halves(value):
    high = value.astype(BF16).astype(F32)
    return high, (value - high).astype(BF16).astype(F32)


def kernel(
    count,
    seqs,
    hidden,
    in_weight,
    dt_weight,
    conv_weight,
    dt_bias,
    decay_rate,
    skip_gain,
    norm_gain,
    out_weight,
    out,
    ext,
    act,
    local,
    gate,
    state,
    scores,
    head_rows,
    cum_cols,
    factors,
    spread_to,
    skip,
    halo,
    came,
    gone,
    halo_send,
    halo_recv,
    send_sem,
    recv_sem,
):
    me = lax.axis_index("seq")
    strand = lax.axis_index("mp")
    before, after = me > 0, me < count - 1
    has_source = (before, after)
    has_target = (after, before)
    target = (me + 1, me - 1)
    which = (strand, 1 - strand)

    barrier = pltpu.get_barrier_semaphore()

    @pl.when(before)
    def _():
        pl.semaphore_signal(barrier, inc=1, device_id={"seq": me - 1}, device_id_type=MESH)

    @pl.when(after)
    def _():
        pl.semaphore_signal(barrier, inc=1, device_id={"seq": me + 1}, device_id_type=MESH)

    inside = before & after

    @pl.when(inside)
    def _():
        pl.semaphore_wait(barrier, 2)

    @pl.when(jnp.logical_not(inside))
    def _():
        pl.semaphore_wait(barrier, 1)

    def halo_copy(d):
        first = ROWS - HALO if d == 0 else 0
        return pltpu.make_async_remote_copy(
            src_ref=hidden.at[:, pl.ds(first, HALO), :],
            dst_ref=halo.at[d],
            send_sem=halo_send.at[d],
            recv_sem=halo_recv.at[d],
            device_id={"seq": target[d]},
            device_id_type=MESH,
        )

    def chain_copy(d, i):
        return pltpu.make_async_remote_copy(
            src_ref=gone.at[d, i],
            dst_ref=came.at[d, i],
            send_sem=send_sem.at[d, i],
            recv_sem=recv_sem.at[d, i],
            device_id={"seq": target[d]},
            device_id_type=MESH,
        )

    for d in range(2):

        @pl.when(has_target[d])
        def _():
            halo_copy(d).start()

        @pl.when(jnp.logical_not(has_source[d]))
        def _():
            halo[d] = jnp.zeros(halo.shape[1:], BF16)
            came[d] = jnp.zeros(came.shape[1:], BF16)

    group_row = lax.broadcasted_iota(jnp.int32, (128, INNER), 0)
    lane_head = lax.broadcasted_iota(jnp.int32, (128, INNER), 1) // HEAD_DIM
    for kind in range(4):
        pick = (group_row == lane_head + 2 * kind * HEADS) | (
            group_row == lane_head + (2 * kind + 1) * HEADS
        )
        spread_to[kind] = jnp.where(pick, 1.0, 0.0).astype(BF16)
    head_pick = jnp.where(
        lax.broadcasted_iota(jnp.int32, (HEADS, INNER), 0)
        == lax.broadcasted_iota(jnp.int32, (HEADS, INNER), 1) // HEAD_DIM,
        1.0,
        0.0,
    )
    for d in range(2):
        row = jnp.broadcast_to(skip_gain[pl.ds(which[d], 1), :], (8, HEADS))
        skip[d] = dot(row, head_pick, precision=HIGHEST)

    row_id = lax.broadcasted_iota(jnp.int32, (ROWS, ROWS), 0)
    col_id = lax.broadcasted_iota(jnp.int32, (ROWS, ROWS), 1)

    def project(b, carry):
        mixed = dot(hidden[b], in_weight[:, INNER:])
        ext[b, pl.ds(8, ROWS), :] = mixed.astype(BF16).astype(F32)
        raw = dot(dt_weight[...], hidden[b], ((0,), (1,)))
        groups, cums = [], []
        for d in range(2):
            biased = raw + column(dt_bias[pl.ds(which[d], 1), :])
            step = jnp.maximum(biased, 0.0) + jnp.log1p(jnp.exp(-jnp.abs(biased)))
            log_decay = -step * column(decay_rate[pl.ds(which[d], 1), :])
            order = (row_id <= col_id) if d == 0 else (row_id >= col_id)
            cum = dot(log_decay, jnp.where(order, 1.0, 0.0), precision=HIGHEST)
            total = cum[:, ROWS - 1 :] if d == 0 else cum[:, :1]
            for c in range(CHUNKS):
                mine = slice(c * CHUNK_HEADS, (c + 1) * CHUNK_HEADS)
                head_rows[b, c, d] = jnp.concatenate([cum[mine], step[mine]], axis=0)
            cums.append(cum)
            groups += [*halves(jnp.exp(cum)), *halves(jnp.exp(total - cum) * step)]
        factors[b] = jnp.transpose(jnp.concatenate(groups, axis=0)).astype(BF16)
        cums.append(jnp.zeros((128 - 2 * HEADS, ROWS), F32))
        cols = jnp.transpose(jnp.concatenate(cums, axis=0))
        for c in range(CHUNKS):
            cum_cols[b, c] = cols if c == 0 else pltpu.roll(cols, 128 - c * CHUNK_HEADS, 1)
        return carry

    lax.fori_loop(0, seqs, project, 0)

    for d in range(2):

        @pl.when(has_source[d])
        def _():
            halo_copy(d).wait_recv()

        edge = dot(halo[d].reshape(seqs * HALO, halo.shape[3]), in_weight[:, INNER:])
        edge = edge.astype(BF16).astype(F32)
        for b in range(seqs):
            if d == 0:
                ext[b, pl.ds(0, 8), :] = edge[b * HALO + HALO - 8 : b * HALO + HALO]
            else:
                ext[b, pl.ds(8 + ROWS, 8), :] = edge[b * HALO : b * HALO + 8]

    def states(b, carry):
        for d in range(2):
            taps = conv_weight[which[d]]
            for first in range(0, MIXED, STATE):
                lanes = pl.ds(first, STATE)
                total = None
                for k in range(CONV):
                    start = 8 - (CONV - 1) + k if d == 0 else 8 + (CONV - 1) - k
                    term = taps[k : k + 1, first : first + STATE] * ext[b, pl.ds(start, ROWS), lanes]
                    total = term if total is None else total + term
                act[d, b, :, lanes] = silu(total).astype(BF16)
            b_part = act[d, b, :, pl.ds(INNER, STATE)]
            c_part = act[d, b, :, pl.ds(INNER + STATE, STATE)]
            for c in range(CHUNKS):
                lanes = pl.ds(c * WIDTH, WIDTH)
                remain = dot(factors[b], spread_to[2 * d + 1, :, lanes])
                weighted = (act[d, b, :, lanes].astype(F32) * remain).astype(BF16)
                gain = dot(b_part, weighted, ((0,), (0,)))
                state[d, b * CHUNKS + c] = gain

                @pl.when(jnp.logical_not(has_source[d]) & has_target[d])
                def _():
                    gone[d, b * CHUNKS + c] = gain.astype(BF16)
                    chain_copy(d, b * CHUNKS + c).start()

            causal = (row_id >= col_id) if d == 0 else (row_id <= col_id)
            scores[d, b] = jnp.where(causal, dot(c_part, b_part, ((1,), (1,))), 0.0)
        return carry

    lax.fori_loop(0, seqs, states, 0)

    half = ROWS // 2
    low_lanes = lax.broadcasted_iota(jnp.int32, (half, 2 * HEAD_DIM), 1) < HEAD_DIM

    def chunk(i, carry):
        b, c = i // CHUNKS, i % CHUNKS
        lanes = pl.ds(pl.multiple_of(c * WIDTH, WIDTH), WIDTH)
        for d in range(2):

            @pl.when(has_source[d])
            def _():
                chain_copy(d, i).wait_recv()

            @pl.when(has_source[d] & has_target[d])
            def _():
                last = 240 if d == 0 else 0
                decay = dot(factors[b, pl.ds(last, 16), :], spread_to[2 * d, :, lanes])
                decay = decay[15:16] if d == 0 else decay[0:1]
                gone[d, i] = (decay * came[d, i].astype(F32) + state[d, i]).astype(BF16)
                chain_copy(d, i).start()

        gate[b, :, lanes] = silu(dot(hidden[b], in_weight[:, lanes]))
        cols = cum_cols[b, c]
        for d in range(2):
            entering = dot(act[d, b, :, pl.ds(INNER + STATE, STATE)], came[d, i])
            entering = entering * dot(factors[b], spread_to[2 * d, :, lanes])
            x_chunk = act[d, b, :, lanes]
            rows = head_rows[b, c, d]
            base = entering + skip[d, 0:1, lanes] * x_chunk.astype(F32)
            for pair in range(CHUNK_HEADS // 2):
                inner = slice(pair * 128, pair * 128 + 128)
                x_pair = x_chunk[:, inner]
                pair_lanes = pl.ds(pl.multiple_of(c * WIDTH + pair * 128, 128), 128)
                for block in range(2):
                    t_rows = slice(block * half, block * half + half)
                    if d == 0:
                        s_rows = slice(0, half + block * half)
                    else:
                        s_rows = slice(block * half, ROWS)
                    tile = scores[d, b, t_rows, s_rows]
                    parts = []
                    for one in range(2):
                        head = pair * 2 + one
                        cum_s = rows[head : head + 1, s_rows]
                        dt_s = rows[CHUNK_HEADS + head : CHUNK_HEADS + head + 1, s_rows]
                        lane = d * HEADS + head
                        cum_t = cols[t_rows, lane : lane + 1]
                        mixing = tile * jnp.exp(jnp.minimum(cum_t - cum_s, 0.0)) * dt_s
                        parts.append(dot(mixing.astype(BF16), x_pair[s_rows]))
                    within = jnp.where(low_lanes, parts[0], parts[1])
                    local[d, b, t_rows, pair_lanes] = within + base[t_rows, inner]

        @pl.when(c == CHUNKS - 1)
        def _():
            for first in range(0, ROWS, 64):
                rows = pl.ds(first, 64)
                silu_gate = gate[b, rows, :]
                summed = None
                for d in range(2):
                    gated = local[d, b, rows, :] * silu_gate
                    mean = jnp.mean(gated * gated, axis=-1, keepdims=True)
                    gated = gated * lax.rsqrt(mean + epsilon) * norm_gain[pl.ds(which[d], 1), :]
                    summed = gated if summed is None else summed + gated
                out[b, rows, :] = dot(summed.astype(BF16), out_weight[...]).astype(BF16)

        return carry

    lax.fori_loop(0, seqs * CHUNKS, chunk, 0)

    for d in range(2):

        @pl.when(has_target[d])
        def _():
            halo_copy(d).wait_send()

            def drain(i, carry):
                chain_copy(d, i).wait_send()
                return carry

            lax.fori_loop(0, seqs * CHUNKS, drain, 0)


def on_device(hidden, *params):
    count = lax.axis_size("seq")
    seqs, rows, width = hidden.shape
    steps = seqs * CHUNKS
    vmem = pl.BlockSpec(memory_space=pltpu.VMEM)
    return pl.pallas_call(
        functools.partial(kernel, count, seqs),
        out_shape=jax.ShapeDtypeStruct((seqs, rows, params[-1].shape[1]), BF16),
        in_specs=[vmem] * 9,
        out_specs=vmem,
        scratch_shapes=[
            pltpu.VMEM((seqs, rows + 16, MIXED), F32),
            pltpu.VMEM((2, seqs, rows, MIXED), BF16),
            pltpu.VMEM((2, seqs, rows, INNER), F32),
            pltpu.VMEM((seqs, rows, INNER), F32),
            pltpu.VMEM((2, steps, STATE, WIDTH), F32),
            pltpu.VMEM((2, seqs, rows, rows), F32),
            pltpu.VMEM((seqs, CHUNKS, 2, 2 * CHUNK_HEADS, rows), F32),
            pltpu.VMEM((seqs, CHUNKS, rows, 128), F32),
            pltpu.VMEM((seqs, rows, 128), BF16),
            pltpu.VMEM((4, 128, INNER), BF16),
            pltpu.VMEM((2, 8, INNER), F32),
            pltpu.VMEM((2, seqs, HALO, width), BF16),
            pltpu.VMEM((2, steps, STATE, WIDTH), BF16),
            pltpu.VMEM((2, steps, STATE, WIDTH), BF16),
            pltpu.SemaphoreType.DMA((2,)),
            pltpu.SemaphoreType.DMA((2,)),
            pltpu.SemaphoreType.DMA((2, steps)),
            pltpu.SemaphoreType.DMA((2, steps)),
        ],
        compiler_params=pltpu.CompilerParams(
            collective_id=0, has_side_effects=True, vmem_limit_bytes=48 * 1024 * 1024
        ),
        name="mixer",
    )(hidden, *params)


def solution(mesh):
    in_specs = (P("groups", "seq", None), P(), P(), P(), P(), P(), P(), P(), P())
    out_specs = P("groups", "seq", "mp")
    return jax.shard_map(
        on_device, mesh=mesh, in_specs=in_specs, out_specs=out_specs, check_vma=False
    )
```

time: 462 us -> 337 us (0.73)
  Pallas kernels: 0 us -> 322 us
  waiting for transfers between devices: 242 us -> 0 us
  local copies, waits for them, and re-layouts: 70.5 us -> 9.07 us
  other arithmetic: 43.6 us -> 0 us
  blocking collectives: 36.3 us -> 0 us
  matrix products: 34.8 us -> 0 us
  between operations: 14 us -> 0.03 us
  starting transfers between devices: 13.1 us -> 0 us
    pallas_call x0 -> x1, Pallas kernels: none -> 322 us  [on_device(): pl.pallas_call(functools.partial(kernel, count, seqs), out_shape=jax.Shap...]
    all_gather x2 -> x0, waiting for transfers between devices: 151 us -> none  [entering(): pieces = jax.tree.map(lambda part: lax.all_gather(part, axis), value)]
    ppermute x8 -> x0, waiting for transfers between devices: 91.6 us -> none  [the longest x6 88.4 us: swapped(): lax.ppermute(shard, axis, [(i, i ^ 1 << bit) for i in range(lax.axis_size...]
    rev x7 -> x0, local copies, waits for them, and re-layouts: 54.5 us -> none  [the longest x1 28.1 us: on_device(): ordered = padded if direction == 0 else padded[:, ::-1]]
    all_gather x2 -> x0, blocking collectives: 36.3 us -> none  [entering(): pieces = jax.tree.map(lambda part: lax.all_gather(part, axis), value)]
    dot_general x13 -> x0, matrix products: 34.8 us -> none  [the longest x2 9.62 us: advance(): jnp.einsum('hts,shp->thp', mixing, heads_x, preferred_element_type=jnp.fl...]
    select_n x15 -> x0, other arithmetic: 21.7 us -> none  [the longest x14 20.8 us: hop(): jnp.where(position < mine, new, old)]
    ppermute x8 -> x0, starting transfers between devices: 13 us -> none  [the longest x6 7.2 us: swapped(): lax.ppermute(shard, axis, [(i, i ^ 1 << bit) for i in range(lax.axis_size...]
  transfers between devices with their start and end apart: 10 -> 0, of which waited for: 9 -> 0; matrix products, arithmetic and copies ran while one was open for 15% -> 0% of each run, Pallas kernels for 0% -> 0%
where the time goes in v1:
time: 337 us; the launch traced here: 332 us
  Pallas kernels  322 us (96%)
  local copies, waits for them, and re-layouts  9.07 us (3%)
    pallas_call x1, Pallas kernels, on_device(): pl.pallas_call(functools.partial(kernel, count, seqs), out_shape=jax.Shap...  322 us
    unnamed x18, local copies, waits for them, and re-layouts  9.07 us

profile of v1, /device:TPU:4, one launch (start us, length us, event | category | flops | bytes accessed | tf_op | source)
XLA Modules:
  0.0 331.6 jit_solution(12068665188272715423)
XLA Ops:
  0.0 0.8 copy.10.dt_weight
  0.8 0.0 copy-start
  0.9 1.7 copy-done
  2.5 0.0 copy-start.1
  2.5 1.2 copy-done.1
  3.7 0.0 copy-start.2
  3.7 1.0 copy-done.2
  4.8 0.0 copy-start.3
  4.8 0.8 copy-done.3
  5.6 0.0 copy-start.4
  5.6 0.7 copy-done.4
  6.3 0.0 copy-start.5
  6.3 0.7 copy-done.5
  6.9 0.0 copy-start.6
  6.9 0.7 copy-done.6
  7.6 0.0 copy-start.7
  7.6 0.7 copy-done.7
  8.3 322.5 %mixer.1 = bf16[2,256,512]{2,1,0:T(8,128)(2,1)S(1)} custom-call(bf16[2,256,512]{2,1,0:T(8,128)(2,1)S(1)} %copy-done.2, bf16[512,2304]{1,0:T(8,128)(2,1)S(1)} %copy-done, bf16[512,16]{1,0:T(8,128)(2,1)S(1)} %copy.10.dt_weight, f32[2,4,1280]{2,1,0:T(4,128)S(1)} %copy-done.3, f32[2,16]{1,0:T(2,128)S(1)} %copy-done.5, f32[2,16]{1,0:T(2,128)S(1)} %copy-done.6, ...), custom_call_target="tpu_custom_call" | custom-call | tf_op jit(solution)/shard_map/mixer/pallas_call | solution.py:318
  330.8 0.8 copy.12
Async XLA Ops:
  0.8 1.7 copy-start
  2.5 1.2 copy-start.1
  3.7 1.0 copy-start.2
  4.8 0.8 copy-start.3
  5.6 0.7 copy-start.4
  6.3 0.7 copy-start.5
  6.9 0.7 copy-start.6
  7.6 0.7 copy-start.7

commit v2 on v1

--- a/solution.py
+++ b/solution.py
@@ -232,31 +232,39 @@
     half = ROWS // 2
     low_lanes = lax.broadcasted_iota(jnp.int32, (half, 2 * HEAD_DIM), 1) < HEAD_DIM
 
-    def chunk(i, carry):
+    steps = seqs * CHUNKS
+
+    def advance(d, i):
         b, c = i // CHUNKS, i % CHUNKS
         lanes = pl.ds(pl.multiple_of(c * WIDTH, WIDTH), WIDTH)
-        for d in range(2):
-
-            @pl.when(has_source[d])
-            def _():
-                chain_copy(d, i).wait_recv()
-
-            @pl.when(has_source[d] & has_target[d])
-            def _():
-                last = 240 if d == 0 else 0
-                decay = dot(factors[b, pl.ds(last, 16), :], spread_to[2 * d, :, lanes])
-                decay = decay[15:16] if d == 0 else decay[0:1]
-                gone[d, i] = (decay * came[d, i].astype(F32) + state[d, i]).astype(BF16)
-                chain_copy(d, i).start()
-
+
+        @pl.when(has_source[d])
+        def _():
+            chain_copy(d, i).wait_recv()
+
+        @pl.when(has_source[d] & has_target[d])
+        def _():
+            last = ROWS - 16 if d == 0 else 0
+            decay = dot(factors[b, pl.ds(last, 16), :], spread_to[2 * d, :, lanes])
+            decay = decay[15:16] if d == 0 else decay[0:1]
+            gone[d, i] = (decay * came[d, i].astype(F32) + state[d, i]).astype(BF16)
+            chain_copy(d, i).start()
+
+    def enter(d, i):
+        b, c = i // CHUNKS, i % CHUNKS
+        lanes = pl.ds(pl.multiple_of(c * WIDTH, WIDTH), WIDTH)
+        entering = dot(act[d, b, :, pl.ds(INNER + STATE, STATE)], came[d, i])
+        local[d, b, :, lanes] += entering * dot(factors[b], spread_to[2 * d, :, lanes])
+
+    def inside_block(i):
+        b, c = i // CHUNKS, i % CHUNKS
+        lanes = pl.ds(pl.multiple_of(c * WIDTH, WIDTH), WIDTH)
         gate[b, :, lanes] = silu(dot(hidden[b], in_weight[:, lanes]))
         cols = cum_cols[b, c]
         for d in range(2):
-            entering = dot(act[d, b, :, pl.ds(INNER + STATE, STATE)], came[d, i])
-            entering = entering * dot(factors[b], spread_to[2 * d, :, lanes])
             x_chunk = act[d, b, :, lanes]
             rows = head_rows[b, c, d]
-            base = entering + skip[d, 0:1, lanes] * x_chunk.astype(F32)
+            base = skip[d, 0:1, lanes] * x_chunk.astype(F32)
             for pair in range(CHUNK_HEADS // 2):
                 inner = slice(pair * 128, pair * 128 + 128)
                 x_pair = x_chunk[:, inner]
@@ -280,22 +288,48 @@
                     within = jnp.where(low_lanes, parts[0], parts[1])
                     local[d, b, t_rows, pair_lanes] = within + base[t_rows, inner]
 
-        @pl.when(c == CHUNKS - 1)
-        def _():
-            for first in range(0, ROWS, 64):
-                rows = pl.ds(first, 64)
-                silu_gate = gate[b, rows, :]
-                summed = None
-                for d in range(2):
-                    gated = local[d, b, rows, :] * silu_gate
-                    mean = jnp.mean(gated * gated, axis=-1, keepdims=True)
-                    gated = gated * lax.rsqrt(mean + epsilon) * norm_gain[pl.ds(which[d], 1), :]
-                    summed = gated if summed is None else summed + gated
-                out[b, rows, :] = dot(summed.astype(BF16), out_weight[...]).astype(BF16)
+    def finish(b):
+        for first in range(0, ROWS, 64):
+            rows = pl.ds(first, 64)
+            silu_gate = gate[b, rows, :]
+            summed = None
+            for d in range(2):
+                gated = local[d, b, rows, :] * silu_gate
+                mean = jnp.mean(gated * gated, axis=-1, keepdims=True)
+                gated = gated * lax.rsqrt(mean + epsilon) * norm_gain[pl.ds(which[d], 1), :]
+                summed = gated if summed is None else summed + gated
+            out[b, rows, :] = dot(summed.astype(BF16), out_weight[...]).astype(BF16)
+
+    hops = (me, count - 1 - me)
+    latest = jnp.maximum(hops[0], hops[1])
+
+    def tick(t, carry):
+        here = [(t >= hops[d]) & (t < hops[d] + steps) for d in range(2)]
+        for d in range(2):
+
+            @pl.when(here[d])
+            def _():
+                advance(d, t - hops[d])
+
+        @pl.when(t < steps)
+        def _():
+            inside_block(t)
+
+        for d in range(2):
+
+            @pl.when(here[d])
+            def _():
+                enter(d, t - hops[d])
+
+        done = t - latest + 1
+
+        @pl.when((done > 0) & (done % CHUNKS == 0) & (done <= steps))
+        def _():
+            finish(done // CHUNKS - 1)
 
         return carry
 
-    lax.fori_loop(0, seqs * CHUNKS, chunk, 0)
+    lax.fori_loop(0, latest + steps, tick, 0)
 
     for d in range(2):
 

time: 337 us -> 80.6 us (0.24)
  the two profiles are of different devices: /device:TPU:4 before, /device:TPU:0 now
where the time goes in v2:
time: 80.6 us; the launch traced here: 80.2 us
  Pallas kernels  71.1 us (88%)
  local copies, waits for them, and re-layouts  9.07 us (11%)
    pallas_call x1, Pallas kernels, on_device(): pl.pallas_call(functools.partial(kernel, count, seqs), out_shape=jax.Shap...  71.1 us
    unnamed x18, local copies, waits for them, and re-layouts  9.07 us

profile of v2, /device:TPU:0, one launch (start us, length us, event | category | flops | bytes accessed | tf_op | source)
XLA Modules:
  0.0 80.2 jit_solution(17958759740642833150)
XLA Ops:
  0.0 0.8 %copy.10.dt_weight = bf16[512,16]{1,0:T(8,128)(2,1)S(1)} copy(bf16[512,16]{0,1:T(8,128)(2,1)} %param.11) | data formatting | bytes 32768 | tf_op args[2]
  0.8 0.0 copy-start
  0.9 1.7 %copy-done = bf16[512,2304]{1,0:T(8,128)(2,1)S(1)} copy-done((bf16[512,2304]{1,0:T(8,128)(2,1)S(1)}, bf16[512,2304]{1,0:T(8,128)(2,1)}, u32[]{:S(2)}) %copy-start) | copy-done | bytes 2359320
  2.5 0.0 copy-start.1
  2.5 1.2 %copy-done.1 = bf16[1024,512]{1,0:T(8,128)(2,1)S(1)} copy-done((bf16[1024,512]{1,0:T(8,128)(2,1)S(1)}, bf16[1024,512]{1,0:T(8,128)(2,1)}, u32[]{:S(2)}) %copy-start.1) | copy-done | bytes 1048600
  3.7 0.0 copy-start.2
  3.7 1.0 %copy-done.2 = bf16[2,256,512]{2,1,0:T(8,128)(2,1)S(1)} copy-done((bf16[2,256,512]{2,1,0:T(8,128)(2,1)S(1)}, bf16[2,256,512]{2,1,0:T(8,128)(2,1)}, u32[]{:S(2)}) %copy-start.2) | copy-done | bytes 524312
  4.8 0.0 copy-start.3
  4.8 0.8 copy-done.3
  5.6 0.0 copy-start.4
  5.6 0.7 copy-done.4
  6.3 0.0 copy-start.5
  6.3 0.7 copy-done.5
  6.9 0.0 copy-start.6
  6.9 0.7 copy-done.6
  7.6 0.0 copy-start.7
  7.6 0.7 copy-done.7
  8.3 71.1 %mixer.1 = bf16[2,256,512]{2,1,0:T(8,128)(2,1)S(1)} custom-call(bf16[2,256,512]{2,1,0:T(8,128)(2,1)S(1)} %copy-done.2, bf16[512,2304]{1,0:T(8,128)(2,1)S(1)} %copy-done, bf16[512,16]{1,0:T(8,128)(2,1)S(1)} %copy.10.dt_weight, f32[2,4,1280]{2,1,0:T(4,128)S(1)} %copy-done.3, f32[2,16]{1,0:T(2,128)S(1)} %copy-done.5, f32[2,16]{1,0:T(2,128)S(1)} %copy-done.6, ...), custom_call_target="tpu_custom_call" | custom-call | tf_op jit(solution)/shard_map/mixer/pallas_call | solution.py:352
  79.4 0.8 copy.12
Async XLA Ops:
  0.8 1.7 %copy-start = (bf16[512,2304]{1,0:T(8,128)(2,1)S(1)}, bf16[512,2304]{1,0:T(8,128)(2,1)}, u32[]{:S(2)}) copy-start(bf16[512,2304]{1,0:T(8,128)(2,1)} %in_weight.1) | copy-start | bytes 7077892
  2.5 1.2 %copy-start.1 = (bf16[1024,512]{1,0:T(8,128)(2,1)S(1)}, bf16[1024,512]{1,0:T(8,128)(2,1)}, u32[]{:S(2)}) copy-start(bf16[1024,512]{1,0:T(8,128)(2,1)} %out_weight.1) | copy-start | bytes 3145732
  3.7 1.0 %copy-start.2 = (bf16[2,256,512]{2,1,0:T(8,128)(2,1)S(1)}, bf16[2,256,512]{2,1,0:T(8,128)(2,1)}, u32[]{:S(2)}) copy-start(bf16[2,256,512]{2,1,0:T(8,128)(2,1)} %hidden.1) | copy-start | bytes 1572868
  4.8 0.8 copy-start.3
  5.6 0.7 copy-start.4
  6.3 0.7 copy-start.5
  6.9 0.7 copy-start.6
  7.6 0.7 copy-start.7

commit v3 on v2

--- a/solution.py
+++ b/solution.py
@@ -14,7 +14,7 @@
 INNER = 1024
 MIXED = INNER + 2 * STATE
 ROWS = 256
-CHUNKS = 4
+CHUNKS = 2
 CHUNK_HEADS = HEADS // CHUNKS
 WIDTH = INNER // CHUNKS
 HALO = 16
@@ -27,7 +27,8 @@
 
 
 def silu(value):
-    return value / (1.0 + jnp.exp(-value))
+    half = 0.5 * value
+    return half + half * jnp.tanh(half)
 
 
 def dot(a, b, dims=((1,), (0,)), precision=None):
@@ -49,6 +50,16 @@
 def kernel(
     count,
     seqs,
+    hidden_hbm,
+    in_weight_hbm,
+    dt_weight_hbm,
+    conv_weight_hbm,
+    dt_bias_hbm,
+    decay_rate_hbm,
+    skip_gain_hbm,
+    norm_gain_hbm,
+    out_weight_hbm,
+    out,
     hidden,
     in_weight,
     dt_weight,
@@ -58,7 +69,6 @@
     skip_gain,
     norm_gain,
     out_weight,
-    out,
     ext,
     act,
     local,
@@ -71,13 +81,38 @@
     spread_to,
     skip,
     halo,
+    pair_out,
+    pair_in,
+    inbox,
     came,
     gone,
     halo_send,
     halo_recv,
+    pair_send,
+    pair_recv,
     send_sem,
     recv_sem,
+    load_sem,
 ):
+    loads = [
+        pltpu.make_async_copy(source, kept, load_sem.at[at])
+        for at, (source, kept) in enumerate(
+            [
+                (hidden_hbm, hidden),
+                (dt_weight_hbm, dt_weight),
+                (in_weight_hbm.at[:, pl.ds(INNER, MIXED)], in_weight.at[:, pl.ds(INNER, MIXED)]),
+                (dt_bias_hbm, dt_bias),
+                (decay_rate_hbm, decay_rate),
+                (skip_gain_hbm, skip_gain),
+                (conv_weight_hbm, conv_weight),
+                (norm_gain_hbm, norm_gain),
+                (in_weight_hbm.at[:, pl.ds(0, INNER)], in_weight.at[:, pl.ds(0, INNER)]),
+                (out_weight_hbm, out_weight),
+            ]
+        )
+    ]
+    for load in loads:
+        load.start()
     me = lax.axis_index("seq")
     strand = lax.axis_index("mp")
     before, after = me > 0, me < count - 1
@@ -86,30 +121,25 @@
     target = (me + 1, me - 1)
     which = (strand, 1 - strand)
 
+    pairs = count // 2
+    odd = me % 2
+    leads = (odd == 1, odd == 0)
+    rank = (me // 2, pairs - 1 - me // 2)
+    partner = me + 1 - 2 * odd
+
     barrier = pltpu.get_barrier_semaphore()
-
-    @pl.when(before)
-    def _():
-        pl.semaphore_signal(barrier, inc=1, device_id={"seq": me - 1}, device_id_type=MESH)
-
-    @pl.when(after)
-    def _():
-        pl.semaphore_signal(barrier, inc=1, device_id={"seq": me + 1}, device_id_type=MESH)
-
-    inside = before & after
-
-    @pl.when(inside)
-    def _():
-        pl.semaphore_wait(barrier, 2)
-
-    @pl.when(jnp.logical_not(inside))
-    def _():
-        pl.semaphore_wait(barrier, 1)
+    for offset in (-2, -1, 1, 2):
+
+        @pl.when((me + offset >= 0) & (me + offset < count))
+        def _():
+            pl.semaphore_signal(barrier, inc=1, device_id={"seq": me + offset}, device_id_type=MESH)
+
+    pl.semaphore_wait(barrier, jnp.minimum(me, 2) + jnp.minimum(count - 1 - me, 2))
 
     def halo_copy(d):
         first = ROWS - HALO if d == 0 else 0
         return pltpu.make_async_remote_copy(
-            src_ref=hidden.at[:, pl.ds(first, HALO), :],
+            src_ref=hidden_hbm.at[:, pl.ds(first, HALO), :],
             dst_ref=halo.at[d],
             send_sem=halo_send.at[d],
             recv_sem=halo_recv.at[d],
@@ -117,16 +147,41 @@
             device_id_type=MESH,
         )
 
-    def chain_copy(d, i):
+    def pair_copy(i):
         return pltpu.make_async_remote_copy(
-            src_ref=gone.at[d, i],
+            src_ref=pair_out.at[i],
+            dst_ref=pair_in.at[i],
+            send_sem=pair_send.at[i],
+            recv_sem=pair_recv.at[i],
+            device_id={"seq": partner},
+            device_id_type=MESH,
+        )
+
+    def lead_copy(d, i):
+        return pltpu.make_async_remote_copy(
+            src_ref=gone.at[i],
+            dst_ref=inbox.at[i],
+            send_sem=send_sem.at[0, i],
+            recv_sem=recv_sem.at[0, i],
+            device_id={"seq": me + 2 * (1 - 2 * d)},
+            device_id_type=MESH,
+        )
+
+    def share_copy(d, i):
+        return pltpu.make_async_remote_copy(
+            src_ref=inbox.at[i],
             dst_ref=came.at[d, i],
-            send_sem=send_sem.at[d, i],
-            recv_sem=recv_sem.at[d, i],
-            device_id={"seq": target[d]},
+            send_sem=send_sem.at[1, i],
+            recv_sem=recv_sem.at[1, i],
+            device_id={"seq": partner},
             device_id_type=MESH,
         )
 
+    def block_decay(d, b, lanes):
+        last = ROWS - 16 if d == 0 else 0
+        decay = dot(factors[b, pl.ds(last, 16), :], spread_to[2 * d, :, lanes])
+        return decay[15:16] if d == 0 else decay[0:1]
+
     for d in range(2):
 
         @pl.when(has_target[d])
@@ -136,7 +191,14 @@
         @pl.when(jnp.logical_not(has_source[d]))
         def _():
             halo[d] = jnp.zeros(halo.shape[1:], BF16)
+
+        @pl.when((rank[d] == 0) & jnp.logical_not(leads[d]))
+        def _():
             came[d] = jnp.zeros(came.shape[1:], BF16)
+
+        @pl.when((rank[d] == 0) & leads[d])
+        def _():
+            inbox[...] = jnp.zeros(inbox.shape, BF16)
 
     group_row = lax.broadcasted_iota(jnp.int32, (128, INNER), 0)
     lane_head = lax.broadcasted_iota(jnp.int32, (128, INNER), 1) // HEAD_DIM
@@ -151,6 +213,8 @@
         1.0,
         0.0,
     )
+    for load in loads[:6]:
+        load.wait()
     for d in range(2):
         row = jnp.broadcast_to(skip_gain[pl.ds(which[d], 1), :], (8, HEADS))
         skip[d] = dot(row, head_pick, precision=HIGHEST)
@@ -161,7 +225,7 @@
     def project(b, carry):
         mixed = dot(hidden[b], in_weight[:, INNER:])
         ext[b, pl.ds(8, ROWS), :] = mixed.astype(BF16).astype(F32)
-        raw = dot(dt_weight[...], hidden[b], ((0,), (1,)))
+        raw = dot(dt_weight[...], hidden[b], ((1,), (1,)))
         groups, cums = [], []
         for d in range(2):
             biased = raw + column(dt_bias[pl.ds(which[d], 1), :])
@@ -210,24 +274,32 @@
                     total = term if total is None else total + term
                 act[d, b, :, lanes] = silu(total).astype(BF16)
             b_part = act[d, b, :, pl.ds(INNER, STATE)]
+            b_turned = jnp.transpose(b_part)
             c_part = act[d, b, :, pl.ds(INNER + STATE, STATE)]
             for c in range(CHUNKS):
                 lanes = pl.ds(c * WIDTH, WIDTH)
                 remain = dot(factors[b], spread_to[2 * d + 1, :, lanes])
                 weighted = (act[d, b, :, lanes].astype(F32) * remain).astype(BF16)
-                gain = dot(b_part, weighted, ((0,), (0,)))
+                gain = dot(b_turned, weighted)
                 state[d, b * CHUNKS + c] = gain
 
-                @pl.when(jnp.logical_not(has_source[d]) & has_target[d])
+                @pl.when(jnp.logical_not(leads[d]))
                 def _():
-                    gone[d, b * CHUNKS + c] = gain.astype(BF16)
-                    chain_copy(d, b * CHUNKS + c).start()
+                    i = b * CHUNKS + c
+                    high, low = halves(block_decay(d, b, lanes))
+                    row = lax.broadcasted_iota(jnp.int32, (16, WIDTH), 0)
+                    pair_out[i, pl.ds(0, STATE), :] = gain.astype(BF16)
+                    pair_out[i, pl.ds(STATE, 16), :] = jnp.where(row == 0, high, low).astype(BF16)
+                    pair_copy(i).start()
 
             causal = (row_id >= col_id) if d == 0 else (row_id <= col_id)
             scores[d, b] = jnp.where(causal, dot(c_part, b_part, ((1,), (1,))), 0.0)
         return carry
 
+    loads[6].wait()
     lax.fori_loop(0, seqs, states, 0)
+    for load in loads[7:]:
+        load.wait()
 
     half = ROWS // 2
     low_lanes = lax.broadcasted_iota(jnp.int32, (half, 2 * HEAD_DIM), 1) < HEAD_DIM
@@ -238,17 +310,27 @@
         b, c = i // CHUNKS, i % CHUNKS
         lanes = pl.ds(pl.multiple_of(c * WIDTH, WIDTH), WIDTH)
 
-        @pl.when(has_source[d])
-        def _():
-            chain_copy(d, i).wait_recv()
-
-        @pl.when(has_source[d] & has_target[d])
-        def _():
-            last = ROWS - 16 if d == 0 else 0
-            decay = dot(factors[b, pl.ds(last, 16), :], spread_to[2 * d, :, lanes])
-            decay = decay[15:16] if d == 0 else decay[0:1]
-            gone[d, i] = (decay * came[d, i].astype(F32) + state[d, i]).astype(BF16)
-            chain_copy(d, i).start()
+        @pl.when((rank[d] > 0) & jnp.logical_not(leads[d]))
+        def _():
+            share_copy(d, i).wait_recv()
+
+        @pl.when(leads[d])
+        def _():
+            @pl.when(rank[d] > 0)
+            def _():
+                lead_copy(d, i).wait_recv()
+                share_copy(d, i).start()
+
+            pair_copy(i).wait_recv()
+            decay = pair_in[i, pl.ds(STATE, 16), :].astype(F32)
+            decay = decay[0:1] + decay[1:2]
+            entry = decay * inbox[i].astype(F32) + pair_in[i, pl.ds(0, STATE), :].astype(F32)
+            came[d, i] = entry.astype(BF16)
+
+            @pl.when(rank[d] < pairs - 1)
+            def _():
+                gone[i] = (block_decay(d, b, lanes) * entry + state[d, i]).astype(BF16)
+                lead_copy(d, i).start()
 
     def enter(d, i):
         b, c = i // CHUNKS, i % CHUNKS
@@ -300,7 +382,7 @@
                 summed = gated if summed is None else summed + gated
             out[b, rows, :] = dot(summed.astype(BF16), out_weight[...]).astype(BF16)
 
-    hops = (me, count - 1 - me)
+    hops = (rank[0] + 1 - odd, rank[1] + odd)
     latest = jnp.maximum(hops[0], hops[1])
 
     def tick(t, carry):
@@ -337,24 +419,42 @@
         def _():
             halo_copy(d).wait_send()
 
-            def drain(i, carry):
-                chain_copy(d, i).wait_send()
+        @pl.when(leads[d] & (rank[d] < pairs - 1))
+        def _():
+            def drain_lead(i, carry):
+                lead_copy(d, i).wait_send()
                 return carry
 
-            lax.fori_loop(0, seqs * CHUNKS, drain, 0)
+            lax.fori_loop(0, steps, drain_lead, 0)
+
+        @pl.when(leads[d] & (rank[d] > 0))
+        def _():
+            def drain_share(i, carry):
+                share_copy(d, i).wait_send()
+                return carry
+
+            lax.fori_loop(0, steps, drain_share, 0)
+
+    def drain_pair(i, carry):
+        pair_copy(i).wait_send()
+        return carry
+
+    lax.fori_loop(0, steps, drain_pair, 0)
 
 
 def on_device(hidden, *params):
     count = lax.axis_size("seq")
     seqs, rows, width = hidden.shape
     steps = seqs * CHUNKS
+    values = (hidden, params[0], params[1].T, *params[2:])
     vmem = pl.BlockSpec(memory_space=pltpu.VMEM)
     return pl.pallas_call(
         functools.partial(kernel, count, seqs),
         out_shape=jax.ShapeDtypeStruct((seqs, rows, params[-1].shape[1]), BF16),
-        in_specs=[vmem] * 9,
+        in_specs=[pl.BlockSpec(memory_space=pl.ANY)] * 9,
         out_specs=vmem,
         scratch_shapes=[
+            *[pltpu.VMEM(value.shape, value.dtype) for value in values],
             pltpu.VMEM((seqs, rows + 16, MIXED), F32),
             pltpu.VMEM((2, seqs, rows, MIXED), BF16),
             pltpu.VMEM((2, seqs, rows, INNER), F32),
@@ -367,18 +467,24 @@
             pltpu.VMEM((4, 128, INNER), BF16),
             pltpu.VMEM((2, 8, INNER), F32),
             pltpu.VMEM((2, seqs, HALO, width), BF16),
+            pltpu.VMEM((steps, STATE + 16, WIDTH), BF16),
+            pltpu.VMEM((steps, STATE + 16, WIDTH), BF16),
+            pltpu.VMEM((steps, STATE, WIDTH), BF16),
             pltpu.VMEM((2, steps, STATE, WIDTH), BF16),
-            pltpu.VMEM((2, steps, STATE, WIDTH), BF16),
+            pltpu.VMEM((steps, STATE, WIDTH), BF16),
             pltpu.SemaphoreType.DMA((2,)),
             pltpu.SemaphoreType.DMA((2,)),
+            pltpu.SemaphoreType.DMA((steps,)),
+            pltpu.SemaphoreType.DMA((steps,)),
             pltpu.SemaphoreType.DMA((2, steps)),
             pltpu.SemaphoreType.DMA((2, steps)),
+            pltpu.SemaphoreType.DMA((10,)),
         ],
         compiler_params=pltpu.CompilerParams(
             collective_id=0, has_side_effects=True, vmem_limit_bytes=48 * 1024 * 1024
         ),
         name="mixer",
-    )(hidden, *params)
+    )(*values)
 
 
 def solution(mesh):

time: 80.6 us -> 57.6 us (0.71)
  the two profiles are of different devices: /device:TPU:0 before, /device:TPU:4 now
where the time goes in v3:
time: 57.6 us; the launch traced here: 57.2 us
  Pallas kernels  48.2 us (84%)
  local copies, waits for them, and re-layouts  8.95 us (16%)
    pallas_call x1, Pallas kernels, on_device(): pl.pallas_call(functools.partial(kernel, count, seqs), out_shape=jax.Shap...  48.2 us
    unnamed x19, local copies, waits for them, and re-layouts  8.95 us

profile of v3, /device:TPU:4, one launch (start us, length us, event | category | flops | bytes accessed | tf_op | source)
XLA Modules:
  0.0 57.2 jit_solution(12075500216492410212)
XLA Ops:
  0.0 0.0 copy-start
  0.0 1.7 %copy-done = bf16[512,2304]{1,0:T(8,128)(2,1)S(1)} copy-done((bf16[512,2304]{1,0:T(8,128)(2,1)S(1)}, bf16[512,2304]{1,0:T(8,128)(2,1)}, u32[]{:S(2)}) %copy-start) | copy-done | bytes 2359320
  1.7 0.0 copy-start.1
  1.7 1.2 %copy-done.1 = bf16[1024,512]{1,0:T(8,128)(2,1)S(1)} copy-done((bf16[1024,512]{1,0:T(8,128)(2,1)S(1)}, bf16[1024,512]{1,0:T(8,128)(2,1)}, u32[]{:S(2)}) %copy-start.1) | copy-done | bytes 1048600
  2.9 0.0 copy-start.2
  2.9 1.0 %copy-done.2 = bf16[2,256,512]{2,1,0:T(8,128)(2,1)S(1)} copy-done((bf16[2,256,512]{2,1,0:T(8,128)(2,1)S(1)}, bf16[2,256,512]{2,1,0:T(8,128)(2,1)}, u32[]{:S(2)}) %copy-start.2) | copy-done | bytes 524312
  3.9 0.0 copy-start.3
  3.9 0.8 %copy-done.3 = f32[2,4,1280]{2,1,0:T(4,128)S(1)} copy-done((f32[2,4,1280]{2,1,0:T(4,128)S(1)}, f32[2,4,1280]{2,1,0:T(4,128)}, u32[]{:S(2)}) %copy-start.3) | copy-done | bytes 40984
  4.7 0.0 copy-start.4
  4.7 0.7 %copy-done.4 = bf16[512,16]{0,1:T(8,128)(2,1)S(1)} copy-done((bf16[512,16]{0,1:T(8,128)(2,1)S(1)}, bf16[512,16]{0,1:T(8,128)(2,1)}, u32[]{:S(2)}) %copy-start.4) | copy-done | bytes 16408
  5.4 0.0 copy-start.5
  5.4 0.7 %copy-done.5 = f32[2,1024]{1,0:T(2,128)S(1)} copy-done((f32[2,1024]{1,0:T(2,128)S(1)}, f32[2,1024]{1,0:T(2,128)}, u32[]{:S(2)}) %copy-start.5) | copy-done | bytes 8216
  6.1 0.0 copy-start.6
  6.1 0.7 %copy-done.6 = f32[2,16]{1,0:T(2,128)S(1)} copy-done((f32[2,16]{1,0:T(2,128)S(1)}, f32[2,16]{1,0:T(2,128)}, u32[]{:S(2)}) %copy-start.6) | copy-done | bytes 152
  6.8 0.0 copy-start.7
  6.8 0.7 %copy-done.7 = f32[2,16]{1,0:T(2,128)S(1)} copy-done((f32[2,16]{1,0:T(2,128)S(1)}, f32[2,16]{1,0:T(2,128)}, u32[]{:S(2)}) %copy-start.7) | copy-done | bytes 152
  7.5 0.0 copy-start.8
  7.5 0.7 %copy-done.8 = f32[2,16]{1,0:T(2,128)S(1)} copy-done((f32[2,16]{1,0:T(2,128)S(1)}, f32[2,16]{1,0:T(2,128)}, u32[]{:S(2)}) %copy-start.8) | copy-done | bytes 152
  8.2 48.2 %mixer.1 = bf16[2,256,512]{2,1,0:T(8,128)(2,1)S(1)} custom-call(bf16[2,256,512]{2,1,0:T(8,128)(2,1)S(1)} %copy-done.2, bf16[512,2304]{1,0:T(8,128)(2,1)S(1)} %copy-done, bf16[16,512]{1,0:T(8,128)(2,1)S(1)} %bitcast.1, f32[2,4,1280]{2,1,0:T(4,128)S(1)} %copy-done.3, f32[2,16]{1,0:T(2,128)S(1)} %copy-done.6, f32[2,16]{1,0:T(2,128)S(1)} %copy-done.7, ...), custom_call_target="tpu_custom_call" | custom-call | tf_op jit(solution)/shard_map/mixer/pallas_call | solution.py:451
  56.4 0.8 %copy.11 = bf16[2,256,512]{2,1,0:T(8,128)(2,1)} copy(bf16[2,256,512]{2,1,0:T(8,128)(2,1)S(1)} %mixer.1) | data formatting | bytes 1048576
Async XLA Ops:
  0.0 1.7 %copy-start = (bf16[512,2304]{1,0:T(8,128)(2,1)S(1)}, bf16[512,2304]{1,0:T(8,128)(2,1)}, u32[]{:S(2)}) copy-start(bf16[512,2304]{1,0:T(8,128)(2,1)} %in_weight_hbm.1) | copy-start | bytes 7077892
  1.7 1.2 %copy-start.1 = (bf16[1024,512]{1,0:T(8,128)(2,1)S(1)}, bf16[1024,512]{1,0:T(8,128)(2,1)}, u32[]{:S(2)}) copy-start(bf16[1024,512]{1,0:T(8,128)(2,1)} %out_weight_hbm.1) | copy-start | bytes 3145732
  2.9 1.0 %copy-start.2 = (bf16[2,256,512]{2,1,0:T(8,128)(2,1)S(1)}, bf16[2,256,512]{2,1,0:T(8,128)(2,1)}, u32[]{:S(2)}) copy-start(bf16[2,256,512]{2,1,0:T(8,128)(2,1)} %hidden_hbm.1) | copy-start | bytes 1572868
  3.9 0.8 %copy-start.3 = (f32[2,4,1280]{2,1,0:T(4,128)S(1)}, f32[2,4,1280]{2,1,0:T(4,128)}, u32[]{:S(2)}) copy-start(f32[2,4,1280]{2,1,0:T(4,128)} %conv_weight_hbm.1) | copy-start | bytes 122884
  4.7 0.7 %copy-start.4 = (bf16[512,16]{0,1:T(8,128)(2,1)S(1)}, bf16[512,16]{0,1:T(8,128)(2,1)}, u32[]{:S(2)}) copy-start(bf16[512,16]{0,1:T(8,128)(2,1)} %param.11) | copy-start | bytes 49156
  5.4 0.7 %copy-start.5 = (f32[2,1024]{1,0:T(2,128)S(1)}, f32[2,1024]{1,0:T(2,128)}, u32[]{:S(2)}) copy-start(f32[2,1024]{1,0:T(2,128)} %norm_gain_hbm.1) | copy-start | bytes 24580
  6.1 0.7 %copy-start.6 = (f32[2,16]{1,0:T(2,128)S(1)}, f32[2,16]{1,0:T(2,128)}, u32[]{:S(2)}) copy-start(f32[2,16]{1,0:T(2,128)} %dt_bias_hbm.1) | copy-start | bytes 388
  6.8 0.7 %copy-start.7 = (f32[2,16]{1,0:T(2,128)S(1)}, f32[2,16]{1,0:T(2,128)}, u32[]{:S(2)}) copy-start(f32[2,16]{1,0:T(2,128)} %decay_rate_hbm.1) | copy-start | bytes 388
  7.5 0.7 %copy-start.8 = (f32[2,16]{1,0:T(2,128)S(1)}, f32[2,16]{1,0:T(2,128)}, u32[]{:S(2)}) copy-start(f32[2,16]{1,0:T(2,128)} %skip_gain_hbm.1) | copy-start | bytes 388

commit v4 on v3

--- a/solution.py
+++ b/solution.py
@@ -310,10 +310,6 @@
         b, c = i // CHUNKS, i % CHUNKS
         lanes = pl.ds(pl.multiple_of(c * WIDTH, WIDTH), WIDTH)
 
-        @pl.when((rank[d] > 0) & jnp.logical_not(leads[d]))
-        def _():
-            share_copy(d, i).wait_recv()
-
         @pl.when(leads[d])
         def _():
             @pl.when(rank[d] > 0)
@@ -335,6 +331,10 @@
     def enter(d, i):
         b, c = i // CHUNKS, i % CHUNKS
         lanes = pl.ds(pl.multiple_of(c * WIDTH, WIDTH), WIDTH)
+        @pl.when((rank[d] > 0) & jnp.logical_not(leads[d]))
+        def _():
+            share_copy(d, i).wait_recv()
+
         entering = dot(act[d, b, :, pl.ds(INNER + STATE, STATE)], came[d, i])
         local[d, b, :, lanes] += entering * dot(factors[b], spread_to[2 * d, :, lanes])
 

time: 57.6 us -> 54.4 us (0.944)
  Pallas kernels: 48.2 us -> 45 us
    pallas_call x1, Pallas kernels: 48.2 us -> 45 us  [on_device(): pl.pallas_call(functools.partial(kernel, count, seqs), out_shape=jax.Shap...]
where the time goes in v4:
time: 54.4 us; the launch traced here: 54 us
  Pallas kernels  45 us (83%)
  local copies, waits for them, and re-layouts  8.95 us (16%)
    pallas_call x1, Pallas kernels, on_device(): pl.pallas_call(functools.partial(kernel, count, seqs), out_shape=jax.Shap...  45 us
    unnamed x19, local copies, waits for them, and re-layouts  8.95 us

profile of v4, /device:TPU:4, one launch (start us, length us, event | category | flops | bytes accessed | tf_op | source)
XLA Modules:
  0.0 54.0 jit_solution(8972809043604966843)
XLA Ops:
  0.0 0.0 copy-start
  0.0 1.7 %copy-done = bf16[512,2304]{1,0:T(8,128)(2,1)S(1)} copy-done((bf16[512,2304]{1,0:T(8,128)(2,1)S(1)}, bf16[512,2304]{1,0:T(8,128)(2,1)}, u32[]{:S(2)}) %copy-start) | copy-done | bytes 2359320
  1.7 0.0 copy-start.1
  1.7 1.2 %copy-done.1 = bf16[1024,512]{1,0:T(8,128)(2,1)S(1)} copy-done((bf16[1024,512]{1,0:T(8,128)(2,1)S(1)}, bf16[1024,512]{1,0:T(8,128)(2,1)}, u32[]{:S(2)}) %copy-start.1) | copy-done | bytes 1048600
  2.9 0.0 copy-start.2
  2.9 1.0 %copy-done.2 = bf16[2,256,512]{2,1,0:T(8,128)(2,1)S(1)} copy-done((bf16[2,256,512]{2,1,0:T(8,128)(2,1)S(1)}, bf16[2,256,512]{2,1,0:T(8,128)(2,1)}, u32[]{:S(2)}) %copy-start.2) | copy-done | bytes 524312
  3.9 0.0 copy-start.3
  3.9 0.8 %copy-done.3 = f32[2,4,1280]{2,1,0:T(4,128)S(1)} copy-done((f32[2,4,1280]{2,1,0:T(4,128)S(1)}, f32[2,4,1280]{2,1,0:T(4,128)}, u32[]{:S(2)}) %copy-start.3) | copy-done | bytes 40984
  4.7 0.0 copy-start.4
  4.7 0.7 %copy-done.4 = bf16[512,16]{0,1:T(8,128)(2,1)S(1)} copy-done((bf16[512,16]{0,1:T(8,128)(2,1)S(1)}, bf16[512,16]{0,1:T(8,128)(2,1)}, u32[]{:S(2)}) %copy-start.4) | copy-done | bytes 16408
  5.4 0.0 copy-start.5
  5.4 0.7 %copy-done.5 = f32[2,1024]{1,0:T(2,128)S(1)} copy-done((f32[2,1024]{1,0:T(2,128)S(1)}, f32[2,1024]{1,0:T(2,128)}, u32[]{:S(2)}) %copy-start.5) | copy-done | bytes 8216
  6.1 0.0 copy-start.6
  6.1 0.7 %copy-done.6 = f32[2,16]{1,0:T(2,128)S(1)} copy-done((f32[2,16]{1,0:T(2,128)S(1)}, f32[2,16]{1,0:T(2,128)}, u32[]{:S(2)}) %copy-start.6) | copy-done | bytes 152
  6.8 0.0 copy-start.7
  6.8 0.7 %copy-done.7 = f32[2,16]{1,0:T(2,128)S(1)} copy-done((f32[2,16]{1,0:T(2,128)S(1)}, f32[2,16]{1,0:T(2,128)}, u32[]{:S(2)}) %copy-start.7) | copy-done | bytes 152
  7.5 0.0 copy-start.8
  7.5 0.7 %copy-done.8 = f32[2,16]{1,0:T(2,128)S(1)} copy-done((f32[2,16]{1,0:T(2,128)S(1)}, f32[2,16]{1,0:T(2,128)}, u32[]{:S(2)}) %copy-start.8) | copy-done | bytes 152
  8.2 45.0 %mixer.1 = bf16[2,256,512]{2,1,0:T(8,128)(2,1)S(1)} custom-call(bf16[2,256,512]{2,1,0:T(8,128)(2,1)S(1)} %copy-done.2, bf16[512,2304]{1,0:T(8,128)(2,1)S(1)} %copy-done, bf16[16,512]{1,0:T(8,128)(2,1)S(1)} %bitcast.1, f32[2,4,1280]{2,1,0:T(4,128)S(1)} %copy-done.3, f32[2,16]{1,0:T(2,128)S(1)} %copy-done.6, f32[2,16]{1,0:T(2,128)S(1)} %copy-done.7, ...), custom_call_target="tpu_custom_call" | custom-call | tf_op jit(solution)/shard_map/mixer/pallas_call | solution.py:451
  53.2 0.8 %copy.11 = bf16[2,256,512]{2,1,0:T(8,128)(2,1)} copy(bf16[2,256,512]{2,1,0:T(8,128)(2,1)S(1)} %mixer.1) | data formatting | bytes 1048576
Async XLA Ops:
  0.0 1.7 %copy-start = (bf16[512,2304]{1,0:T(8,128)(2,1)S(1)}, bf16[512,2304]{1,0:T(8,128)(2,1)}, u32[]{:S(2)}) copy-start(bf16[512,2304]{1,0:T(8,128)(2,1)} %in_weight_hbm.1) | copy-start | bytes 7077892
  1.7 1.2 %copy-start.1 = (bf16[1024,512]{1,0:T(8,128)(2,1)S(1)}, bf16[1024,512]{1,0:T(8,128)(2,1)}, u32[]{:S(2)}) copy-start(bf16[1024,512]{1,0:T(8,128)(2,1)} %out_weight_hbm.1) | copy-start | bytes 3145732
  2.9 1.0 %copy-start.2 = (bf16[2,256,512]{2,1,0:T(8,128)(2,1)S(1)}, bf16[2,256,512]{2,1,0:T(8,128)(2,1)}, u32[]{:S(2)}) copy-start(bf16[2,256,512]{2,1,0:T(8,128)(2,1)} %hidden_hbm.1) | copy-start | bytes 1572868
  3.9 0.8 %copy-start.3 = (f32[2,4,1280]{2,1,0:T(4,128)S(1)}, f32[2,4,1280]{2,1,0:T(4,128)}, u32[]{:S(2)}) copy-start(f32[2,4,1280]{2,1,0:T(4,128)} %conv_weight_hbm.1) | copy-start | bytes 122884
  4.7 0.7 %copy-start.4 = (bf16[512,16]{0,1:T(8,128)(2,1)S(1)}, bf16[512,16]{0,1:T(8,128)(2,1)}, u32[]{:S(2)}) copy-start(bf16[512,16]{0,1:T(8,128)(2,1)} %param.11) | copy-start | bytes 49156
  5.4 0.7 %copy-start.5 = (f32[2,1024]{1,0:T(2,128)S(1)}, f32[2,1024]{1,0:T(2,128)}, u32[]{:S(2)}) copy-start(f32[2,1024]{1,0:T(2,128)} %norm_gain_hbm.1) | copy-start | bytes 24580
  6.1 0.7 %copy-start.6 = (f32[2,16]{1,0:T(2,128)S(1)}, f32[2,16]{1,0:T(2,128)}, u32[]{:S(2)}) copy-start(f32[2,16]{1,0:T(2,128)} %dt_bias_hbm.1) | copy-start | bytes 388
  6.8 0.7 %copy-start.7 = (f32[2,16]{1,0:T(2,128)S(1)}, f32[2,16]{1,0:T(2,128)}, u32[]{:S(2)}) copy-start(f32[2,16]{1,0:T(2,128)} %decay_rate_hbm.1) | copy-start | bytes 388
  7.5 0.7 %copy-start.8 = (f32[2,16]{1,0:T(2,128)S(1)}, f32[2,16]{1,0:T(2,128)}, u32[]{:S(2)}) copy-start(f32[2,16]{1,0:T(2,128)} %skip_gain_hbm.1) | copy-start | bytes 388
